TPU v7x, 32 devices: a whole 2x2x4 slice. The times are simulated.
32 devices in a mesh: occ: 4 (over y, core), vir: 8 (over z, x).
Axes of the slice: x: 2, y: 2, z: 4, core: 2. Of those that a mesh axis runs over, the one named last changes fastest.
Arguments:
- amplitudes: bfloat16 [64, 64, 4096], P('occ', 'vir'), may hold values from -6 to 6
- screen: int32 [64, 64], P('occ', 'vir'), may hold values 0 or 1
- integrals: bfloat16 [4096, 16384], P(None, 'vir'), as said below
Outputs:
- ladder_residual: bfloat16 [64, 64, 128, 128], P('occ', None, 'vir')
Inputs may be any that keep to these rules, and one draw needn't show every extreme that they name: integrals[(c, d), (a, b)] equals integrals[(d, c), (b, a)] for all a, b, c, d.
All inputs are finite; a program needn't handle non-finite values. No bound on the sum of `screen` on one device may be relied on, other than what follows from the above.
Results may differ from a plain program's by a relative error of at most 0.0075.
Values may be sent and summed in bfloat16 or wider, within the bound.
A program may use at most 256 MiB of HBM per device.

v0:
```python
import jax
import jax.numpy as jnp
from jax import lax
from jax.sharding import PartitionSpec as P

TILE = 64
SLAB_VIRT = 128


def per_device(amplitudes, screen, integrals):
    masked = amplitudes * screen[:, :, None].astype(jnp.bfloat16)
    rows_here = masked.shape[0]
    width = integrals.shape[1]
    slab_full = SLAB_VIRT
    slab_local = width // slab_full
    whole = lax.all_gather(masked, "vir", axis=1, tiled=True)
    occ_all = whole.shape[1]
    swapped = lax.all_to_all(whole, "occ", split_axis=1, concat_axis=0, tiled=True)
    swapped_four = swapped.reshape(occ_all, rows_here, TILE, TILE)
    reversed_pairs = jnp.transpose(swapped_four, (1, 0, 3, 2)).reshape(
        rows_here, occ_all, TILE * TILE
    )
    summed = whole.astype(jnp.float32) + reversed_pairs.astype(jnp.float32)
    upper_part = summed.astype(jnp.bfloat16)
    lower_part = (summed - upper_part.astype(jnp.float32)).astype(jnp.bfloat16)
    joined = jnp.concatenate([upper_part, lower_part], axis=2)
    doubled = jnp.concatenate([integrals, integrals], axis=0)
    combined = jnp.einsum("ijc,cn->ijn", joined, doubled, preferred_element_type=jnp.float32)
    total = combined.reshape(rows_here, occ_all, slab_local, slab_full)
    return total.astype(jnp.bfloat16)


def solution(mesh):
    return jax.shard_map(
        per_device,
        mesh=mesh,
        in_specs=(P("occ", "vir", None), P("occ", "vir"), P(None, "vir")),
        out_specs=P("occ", None, "vir", None),
        check_vma=False,
    )
```

profile of v0, /device:TPU:24, one launch (start us, length us, event | category | flops | bytes accessed | tf_op | source)
XLA Modules:
  0.0 409.8 jit_solution(17799418098542192984)
XLA Ops:
  6.5 0.0 all-gather.2.cloned.1.call-start
  6.5 0.7 convert_element_type.37
  7.2 0.1 copy.8
  7.3 2.3 broadcast_multiply_fusion
  9.6 0.0 all-gather.2.cloned.1.call-update
  9.7 124.1 %all-gather.2.cloned.1.call-done = bf16[16,64,4096]{2,1,0:T(8,128)(2,1)} async-done(((bf16[16,8,4096]{2,1,0:T(8,128)(2,1)}), bf16[16,64,4096]{2,1,0:T(8,128)(2,1)}) %all-gather.2.cloned.1.call-update) | async-done | bytes 8388624 | tf_op jit(solution)/shard_map/all_gather | solution.py:16
  133.8 11.2 %copy.9 = bf16[16,64,4096]{2,0,1:T(8,128)(2,1)} copy(bf16[16,64,4096]{2,1,0:T(8,128)(2,1)} %all-gather.2.cloned.1.call-done) | data formatting | bytes 16777216 | tf_op jit(solution)/shard_map/all_gather | solution.py:16
  145.0 100.5 %all_to_all.12 = bf16[16,64,4096]{2,0,1:T(8,128)(2,1)} all-to-all(bf16[16,64,4096]{2,0,1:T(8,128)(2,1)} %copy.9), channel_id=1, replica_groups=mesh['occ'=4,'vir'=8] {'occ'}, dimensions={1} | all-to-all | bytes 16777216 | tf_op jit(solution)/shard_map/all_to_all | solution.py:18
  245.5 14.0 %copy.14 = f32[16,4,16,4096]{3,2,0,1:T(8,128)} copy(bf16[16,4,16,4096]{3,0,2,1:T(8,128)(2,1)} %bitcast.24) | data formatting | bytes 25165824 | tf_op jit(solution)/shard_map/convert_element_type | solution.py:23
  259.5 27.0 %reshape.12 = f32[64,16,64,64]{3,2,1,0:T(8,128)} reshape(f32[4,16,16,4096]{3,2,1,0:T(8,128)} %bitcast.23) | data formatting | bytes 33554432 | tf_op jit(solution)/shard_map/convert_element_type | solution.py:23
  286.6 31.1 %copy.11 = f32[16,64,64,64]{3,2,1,0:T(8,128)} copy(f32[16,64,64,64]{2,3,0,1:T(8,128)} %bitcast.22) | data formatting | bytes 33554432 | tf_op jit(solution)/shard_map/convert_element_type | solution.py:23
  317.7 27.9 %reshape.11 = f32[16,64,4096]{2,1,0:T(8,128)} reshape(f32[16,64,64,64]{3,2,1,0:T(8,128)} %copy.11) | data formatting | bytes 33554432 | tf_op jit(solution)/shard_map/convert_element_type | solution.py:23
  345.6 12.1 %fusion.6 = (bf16[16,64,4096]{2,1,0:T(8,128)(2,1)S(1)}, bf16[16,64,4096]{2,1,0:T(8,128)(2,1)}) fusion(f32[16,64,4096]{2,1,0:T(8,128)} %reshape.11, bf16[16,64,4096]{2,1,0:T(8,128)(2,1)} %all-gather.2.cloned.1.call-done), kind=kLoop, calls=%fused_computation.10 | loop fusion | flops 25165824 | bytes 41943040 | tf_op jit(solution)/shard_map/convert_element_type | solution.py:24
  357.7 41.8 %fusion.7 = bf16[16,64,2048]{2,1,0:T(8,128)(2,1)S(1)} fusion(bf16[4096,2048]{1,0:T(8,128)(2,1)} %param.5, bf16[16,64,4096]{2,1,0:T(8,128)(2,1)} %get-tuple-element.6, bf16[16,64,4096]{2,1,0:T(8,128)(2,1)S(1)} %get-tuple-element.5), kind=kOutput, calls=%fused_computation.11 | convolution fusion | flops 34462498816 | bytes 37748736 | tf_op jit(solution)/shard_map/ijc,cn->ijn/dot_general | solution.py:28
  399.5 3.4 copy.12
Async XLA Ops:
  6.5 127.2 %all-gather.2.cloned.1.call-start = ((), (), s32[]{:S(2)}) async-start(), calls=%async_computation.1 | async-start | bytes 9437184 | tf_op jit(solution)/shard_map/all_gather | solution.py:16
Sparse Core Ops, SparseCore 0:
  9.8 123.9 all-gather.1
where the time goes:
time: 415 us; the launch traced here: 410 us
  waiting for transfers between devices  124 us (30%)
  local copies, waits for them, and re-layouts  115 us (28%)
  blocking collectives  101 us (24%)
  matrix products  41.8 us (10%)
  other arithmetic  15.1 us (4%)
  between operations  13.4 us (3%)
    all_gather x1, waiting for transfers between devices, per_device(): whole = lax.all_gather(masked, 'vir', axis=1, tiled=True)  124 us
    all_to_all x1, blocking collectives, per_device(): lax.all_to_all(whole, 'occ', split_axis=1, concat_axis=0, tiled=True)  101 us
    convert_element_type x4, local copies, waits for them, and re-layouts, per_device(): summed = whole.astype(jnp.float32) + reversed_pairs.astype(jnp.float32)  100 us
    dot_general x1, matrix products, per_device(): jnp.einsum('ijc,cn->ijn', joined, doubled, preferred_element_type=jnp.flo...  41.8 us
    convert_element_type x1, other arithmetic, per_device(): upper_part = summed.astype(jnp.bfloat16)  12.1 us
    all_gather x1, local copies, waits for them, and re-layouts, per_device(): whole = lax.all_gather(masked, 'vir', axis=1, tiled=True)  11.2 us
  transfers between devices with their start and end apart: 1, of which 1 were waited for; matrix products, arithmetic and copies ran while one was open for 0% of the time, Pallas kernels for 0%

commit v1 on v0

v1 whole, which is shorter than its diff:
```python
import jax
import jax.numpy as jnp
from jax import lax
from jax.sharding import PartitionSpec as P

TILE = 64
SLAB_VIRT = 128


def per_device(sizes, amplitudes, screen, integrals):
    n_occ, n_vir = sizes
    masked = amplitudes * screen[:, :, None].astype(jnp.bfloat16)
    rows, cols, cdim = masked.shape
    ratio = rows // cols
    r = lax.rem(lax.axis_index("vir"), ratio)
    parts = masked.reshape(ratio, cols, cols, cdim)
    flipped = jnp.transpose(
        parts.reshape(ratio, cols, cols, TILE, TILE), (0, 2, 1, 4, 3)
    ).reshape(ratio, cols, cols, cdim)
    got = []
    for s in range(ratio):
        pairs = []
        for o in range(n_occ):
            for v in range(n_vir):
                q, rr = divmod(v, ratio)
                pairs.append((o * n_vir + v, q * n_vir + o * ratio + (rr + s) % ratio))
        sent = lax.dynamic_index_in_dim(flipped, lax.rem(r + s, ratio), 0, keepdims=False)
        got.append(lax.ppermute(sent, ("occ", "vir"), pairs))
    stacked = jnp.stack(got)
    order = lax.rem(r - jnp.arange(ratio) + ratio, ratio)
    partner = jnp.take(stacked, order, axis=0)
    local = (parts.astype(jnp.float32) + partner.astype(jnp.float32)).astype(jnp.bfloat16)
    local = local.reshape(rows, cols, cdim)
    whole = lax.all_gather(local, "vir", axis=1, tiled=True)
    out = jnp.einsum("ijc,cn->ijn", whole, integrals, preferred_element_type=jnp.float32)
    return out.astype(jnp.bfloat16).reshape(rows, whole.shape[1], -1, SLAB_VIRT)


def solution(mesh):
    sizes = (mesh.shape["occ"], mesh.shape["vir"])
    return jax.shard_map(
        lambda *args: per_device(sizes, *args),
        mesh=mesh,
        in_specs=(P("occ", "vir", None), P("occ", "vir"), P(None, "vir")),
        out_specs=P("occ", None, "vir", None),
        check_vma=False,
    )
```

time: 415 us -> 232 us (0.56)
  local copies, waits for them, and re-layouts: 115 us -> 13.4 us
  blocking collectives: 101 us -> 0 us
  waiting for transfers between devices: 124 us -> 166 us
  matrix products: 41.8 us -> 22.7 us
  other arithmetic: 15.1 us -> 4.71 us
  starting transfers between devices: 0.01 us -> 7.33 us
    all_to_all x1 -> x0, blocking collectives: 101 us -> none  [per_device(): lax.all_to_all(whole, 'occ', split_axis=1, concat_axis=0, tiled=True)]
    convert_element_type x4 -> x0, local copies, waits for them, and re-layouts: 100 us -> none  [per_device(): summed = whole.astype(jnp.float32) + reversed_pairs.astype(jnp.float32)]
    ppermute x0 -> x2, waiting for transfers between devices: none -> 23.6 us  [per_device(): got.append(lax.ppermute(sent, ('occ', 'vir'), pairs))]
    dot_general x1, matrix products: 41.8 us -> 22.7 us  [per_device(): jnp.einsum('ijc,cn->ijn', whole, integrals, preferred_element_type=jnp.fl...]
    all_gather x1, waiting for transfers between devices: 124 us -> 142 us  [per_device(): whole = lax.all_gather(local, 'vir', axis=1, tiled=True)]
    all_gather x1 -> x0, local copies, waits for them, and re-layouts: 11.2 us -> none  [per_device(): whole = lax.all_gather(masked, 'vir', axis=1, tiled=True)]
    convert_element_type x1, other arithmetic: 12.1 us -> 1.48 us  [per_device(): (parts.astype(jnp.float32) + partner.astype(jnp.float32)).astype(jnp.bflo...]
    ppermute x0 -> x2, starting transfers between devices: none -> 7.33 us  [per_device(): got.append(lax.ppermute(sent, ('occ', 'vir'), pairs))]
  transfers between devices with their start and end apart: 1 -> 3, of which waited for: 1 -> 3; matrix products, arithmetic and copies ran while one was open for 0% -> 0% of each run, Pallas kernels for 0% -> 0%
where the time goes in v1:
time: 232 us; the launch traced here: 228 us
  waiting for transfers between devices  166 us (72%)
  matrix products  22.7 us (10%)
  between operations  13.5 us (6%)
  local copies, waits for them, and re-layouts  13.4 us (6%)
  starting transfers between devices  7.33 us (3%)
  other arithmetic  4.71 us (2%)
    all_gather x1, waiting for transfers between devices, per_device(): whole = lax.all_gather(local, 'vir', axis=1, tiled=True)  142 us
    ppermute x2, waiting for transfers between devices, per_device(): got.append(lax.ppermute(sent, ('occ', 'vir'), pairs))  23.6 us
    dot_general x1, matrix products, per_device(): jnp.einsum('ijc,cn->ijn', whole, integrals, preferred_element_type=jnp.fl...  22.7 us
    ppermute x2, starting transfers between devices, per_device(): got.append(lax.ppermute(sent, ('occ', 'vir'), pairs))  7.33 us
    another operation x2, local copies, waits for them, and re-layouts, per_device(): parts.reshape(ratio, cols, cols, TILE, TILE)  4.89 us
  transfers between devices with their start and end apart: 3, of which 3 were waited for; matrix products, arithmetic and copies ran while one was open for 0% of the time, Pallas kernels for 0%

profile of v1, /device:TPU:24, one launch (start us, length us, event | category | flops | bytes accessed | tf_op | source)
XLA Modules:
  0.0 227.6 jit_solution(3187118220330454654)
XLA Ops:
  6.5 0.0 all-gather.2.cloned.1.call-start
  6.5 0.7 convert_element_type.19
  7.2 0.1 copy.5
  7.3 1.4 broadcast_multiply_fusion
  8.7 2.3 %reshape_reshape.3 = bf16[2,8,8,64,64]{4,3,2,1,0:T(8,128)(2,1)S(1)} reshape(bf16[16,8,4096]{2,1,0:T(8,128)(2,1)S(1)} %broadcast_multiply_fusion) | data formatting | bytes 2097152 | tf_op jit(solution)/shard_map/reshape;reshape | solution.py:18
  11.0 0.0 copy-start
  11.0 2.6 %copy.6 = bf16[2,8,8,64,64]{3,4,1,2,0:T(8,128)(2,1)} copy(bf16[2,8,8,64,64]{4,3,2,1,0:T(8,128)(2,1)S(1)} %reshape_reshape.3) | data formatting | bytes 2097152 | tf_op jit(solution)/shard_map/reshape;reshape | solution.py:18
  13.6 3.3 %reshape.54 = bf16[2,8,8,4096]{3,2,1,0:T(8,128)(2,1)S(1)} reshape(bf16[2,8,8,64,64]{4,3,2,1,0:T(8,128)(2,1)} %bitcast.25) | data formatting | bytes 2097152 | tf_op jit(solution)/shard_map/reshape | solution.py:19
  16.9 0.9 dynamic-slice_bitcast_fusion.1
  17.8 2.5 %collective-permute-start = (bf16[8,8,4096]{2,1,0:T(8,128)(2,1)}, bf16[8,8,4096]{2,1,0:T(8,128)(2,1)S(1)}, u32[]{:S(2)}, u32[]{:S(2)}) collective-permute-start(bf16[8,8,4096]{2,1,0:T(8,128)(2,1)} %get-tuple-element.5), channel_id=1, source_target_pairs={{0,0},{1,1},{2,8},{3,9},{4,16},{5,17},{6,24},{7,25},{8,2},{9,3},{1... | collective-permute-start | bytes 1572872 | tf_op jit(solution)/shard_map/ppermute | solution.py:28
  20.3 4.8 %collective-permute-start.1 = (bf16[8,8,4096]{2,1,0:T(8,128)(2,1)S(1)}, bf16[8,8,4096]{2,1,0:T(8,128)(2,1)}, u32[]{:S(2)}, u32[]{:S(2)}) collective-permute-start(bf16[8,8,4096]{2,1,0:T(8,128)(2,1)S(1)} %get-tuple-element.6), channel_id=1, source_target_pairs={{0,1},{1,0},{2,9},{3,8},{4,17},{5,16},{6,25},{7,24},{8,3},{9,2},{1... | collective-permute-start | bytes 1572872 | tf_op jit(solution)/shard_map/ppermute | solution.py:28
  25.2 0.1 broadcast_in_dim.15
  25.2 0.1 broadcast_in_dim.16
  25.3 11.5 %collective-permute-done = bf16[8,8,4096]{2,1,0:T(8,128)(2,1)S(1)} collective-permute-done((bf16[8,8,4096]{2,1,0:T(8,128)(2,1)}, bf16[8,8,4096]{2,1,0:T(8,128)(2,1)S(1)}, u32[]{:S(2)}, u32[]{:S(2)}) %collective-permute-start) | collective-permute-done | bytes 524320 | tf_op jit(solution)/shard_map/ppermute | solution.py:28
  36.8 12.1 %collective-permute-done.1 = bf16[8,8,4096]{2,1,0:T(8,128)(2,1)} collective-permute-done((bf16[8,8,4096]{2,1,0:T(8,128)(2,1)S(1)}, bf16[8,8,4096]{2,1,0:T(8,128)(2,1)}, u32[]{:S(2)}, u32[]{:S(2)}) %collective-permute-start.1) | collective-permute-done | bytes 524320 | tf_op jit(solution)/shard_map/ppermute | solution.py:28
  48.9 1.1 pad_maximum_fusion
  50.1 0.6 gather_fusion
  50.7 0.0 copy-done
  50.7 1.5 add_convert_fusion
  52.2 0.0 all-gather.2.cloned.1.call-update
  52.2 142.4 %all-gather.2.cloned.1.call-done = bf16[16,64,4096]{2,1,0:T(8,128)(2,1)} async-done(((bf16[16,8,4096]{2,1,0:T(8,128)(2,1)}), bf16[16,64,4096]{2,1,0:T(8,128)(2,1)}) %all-gather.2.cloned.1.call-update) | async-done | bytes 8388624 | tf_op jit(solution)/shard_map/all_gather | solution.py:34
  194.6 22.7 %fusion.2 = bf16[16,64,2048]{2,1,0:T(8,128)(2,1)S(1)} fusion(bf16[16,64,4096]{2,1,0:T(8,128)(2,1)} %all-gather.2.cloned.1.call-done, bf16[4096,2048]{1,0:T(8,128)(2,1)} %param.5), kind=kOutput, calls=%fused_computation.3 | convolution fusion | flops 17181966336 | bytes 29360128 | tf_op jit(solution)/shard_map/ijc,cn->ijn/dot_general | solution.py:35
  217.3 3.4 %copy.7 = bf16[128,8,16,128]{3,2,1,0:T(8,128)(2,1)} copy(bf16[128,8,16,128]{3,1,2,0:T(8,128)(2,1)S(1)} %bitcast.26) | data formatting | bytes 8388608
  (3 shorter events, 0.0 us)
Async XLA Ops:
  6.5 188.1 %all-gather.2.cloned.1.call-start = ((), (), s32[]{:S(2)}) async-start(), calls=%async_computation | async-start | bytes 9437184 | tf_op jit(solution)/shard_map/all_gather | solution.py:34
  11.0 39.7 %copy-start = (bf16[16,8,4096]{2,1,0:T(8,128)(2,1)S(1)}, bf16[16,8,4096]{2,1,0:T(8,128)(2,1)}, u32[]{:S(2)}) copy-start(bf16[16,8,4096]{2,1,0:T(8,128)(2,1)} %param.3) | copy-start | bytes 3145732
  17.8 19.0 %collective-permute-start = (bf16[8,8,4096]{2,1,0:T(8,128)(2,1)}, bf16[8,8,4096]{2,1,0:T(8,128)(2,1)S(1)}, u32[]{:S(2)}, u32[]{:S(2)}) collective-permute-start(bf16[8,8,4096]{2,1,0:T(8,128)(2,1)} %get-tuple-element.5), channel_id=1, source_target_pairs={{0,0},{1,1},{2,8},{3,9},{4,16},{5,17},{6,24},{7,25},{8,2},{9,3},{1... | collective-permute-start | bytes 1572872 | tf_op jit(solution)/shard_map/ppermute | solution.py:28
  20.3 28.6 %collective-permute-start.1 = (bf16[8,8,4096]{2,1,0:T(8,128)(2,1)S(1)}, bf16[8,8,4096]{2,1,0:T(8,128)(2,1)}, u32[]{:S(2)}, u32[]{:S(2)}) collective-permute-start(bf16[8,8,4096]{2,1,0:T(8,128)(2,1)S(1)} %get-tuple-element.6), channel_id=1, source_target_pairs={{0,1},{1,0},{2,9},{3,8},{4,17},{5,16},{6,25},{7,24},{8,3},{9,2},{1... | collective-permute-start | bytes 1572872 | tf_op jit(solution)/shard_map/ppermute | solution.py:28
Sparse Core Ops, SparseCore 0:
  52.3 142.2 all-gather.1

commit v2 on v0

v2 whole, which is shorter than its diff:
```python
import functools

import jax
import jax.numpy as jnp
from jax import lax
from jax.experimental import pallas as pl
from jax.experimental.pallas import tpu as pltpu
from jax.sharding import PartitionSpec as P

TILE = 64
SLAB_VIRT = 128
LINE = 4
CHUNKS = 2
MESH = pl.DeviceIdType.MESH


def exchange_kernel(n_occ, n_vir, main, extra, gathered, turned, local_sem, send_sem, recv_sem, turn_send, turn_recv, extra_send):
    ratio = n_vir // n_occ
    line = LINE if n_vir % LINE == 0 else 1
    wide = n_vir // line
    o, v = lax.axis_index("occ"), lax.axis_index("vir")
    z, x = v // wide, lax.rem(v, wide)
    pairs, cdim = main.shape
    piece = pairs // CHUNKS
    strip = cdim // n_vir
    owner = o * ratio + 1

    barrier = pltpu.get_barrier_semaphore()
    for step in range(1, n_vir):
        pl.semaphore_signal(barrier, inc=1, device_id=(o, lax.rem(v + step, n_vir)), device_id_type=MESH)
    for step in range(1, n_occ):
        pl.semaphore_signal(barrier, inc=1, device_id=(lax.rem(o + step, n_occ), v), device_id_type=MESH)
    pl.semaphore_wait(barrier, n_vir + n_occ - 2)

    def place(source, c):
        if c < CHUNKS:
            return gathered.at[source, pl.ds(c * piece, piece)]
        return gathered.at[n_vir, :, pl.ds(pl.multiple_of(source * strip, strip), strip)]

    def held(source, c, own):
        if own and c < CHUNKS:
            return main.at[pl.ds(c * piece, piece)]
        return place(source, c)

    def along(source, c, own, way, target):
        return pltpu.make_async_remote_copy(
            src_ref=held(source, c, own), dst_ref=place(source, c),
            send_sem=send_sem.at[source, c, way], recv_sem=recv_sem.at[source, c],
            device_id=(o, target), device_id_type=MESH,
        )

    def across(source, c, own):
        return pltpu.make_async_remote_copy(
            src_ref=held(source, c, own),
            dst_ref=turned.at[o, lax.rem(source, ratio), pl.ds(c * piece, piece)],
            send_sem=turn_send.at[source, c],
            recv_sem=turn_recv.at[o, lax.rem(source, ratio), c],
            device_id=(source // ratio, v), device_id_type=MESH,
        )

    waits = []

    def start(cond, make):
        def begin():
            make().start()

        def finish():
            make().wait_send()

        pl.when(cond)(begin)
        waits.append((cond, finish))

    def spread(cond, source, c, own, up, down, sides):
        if up:
            start(cond & (z < line - 1), lambda: along(source, c, own, 0, v + wide))
        if down:
            start(cond & (z > 0), lambda: along(source, c, own, 1, v - wide))
        if sides:
            for step in range(1, wide):
                start(cond, lambda step=step: along(source, c, own, 1 + step, z * wide + lax.rem(x + step, wide)))
        if c < CHUNKS:
            start(cond & (source // ratio != o), lambda: across(source, c, own))

    def arrive(cond, source, c, up, down, sides):
        @pl.when(cond)
        def _():
            along(source, c, False, 0, v).wait_recv()

        spread(cond, source, c, False, up, down, sides)

    always = v >= 0
    keep = pltpu.make_async_copy(main, gathered.at[v], local_sem.at[0])

    def strip_of(target):
        return extra.at[:, pl.ds(pl.multiple_of(target * strip, strip), strip)]

    own_strip = pltpu.make_async_copy(strip_of(v), place(v, CHUNKS), local_sem.at[1])

    def far_strip(step):
        target = lax.rem(v + step, n_vir)
        return pltpu.make_async_remote_copy(
            src_ref=strip_of(target), dst_ref=place(target, CHUNKS),
            send_sem=extra_send.at[step], recv_sem=recv_sem.at[target, CHUNKS],
            device_id=(o, target), device_id_type=MESH,
        )

    for c in range(CHUNKS):
        spread(always, v, c, True, True, True, True)

    @pl.when(v == owner)
    def _():
        own_strip.start()
        for step in range(1, n_vir):
            far_strip(step).start()
        own_strip.wait()

    keep.start()

    @pl.when(v != owner)
    def _():
        along(v, CHUNKS, False, 0, v).wait_recv()

    spread(always, v, CHUNKS, True, True, True, True)

    for d in range(1, line + 1):
        for c in range(CHUNKS + 1):
            if d < line:
                arrive(z >= d, (z - d) * wide + x, c, True, False, True)
                arrive(z < line - d, (z + d) * wide + x, c, False, True, True)
            for step in range(1, wide):
                side = lax.rem(x + step, wide)
                e = d - 1
                arrive(z >= e, (z - e) * wide + side, c, False, False, False)
                if e:
                    arrive(z < line - e, (z + e) * wide + side, c, False, False, False)

    again = pltpu.make_async_copy(gathered.at[n_vir], turned.at[o, 0], local_sem.at[2])
    again.start()
    for step in range(1, n_occ):
        other = lax.rem(o + step, n_occ)
        for k in range(ratio):
            for c in range(CHUNKS):
                pltpu.make_async_remote_copy(
                    src_ref=turned.at[other, k, pl.ds(c * piece, piece)],
                    dst_ref=turned.at[other, k, pl.ds(c * piece, piece)],
                    send_sem=turn_send.at[0, c], recv_sem=turn_recv.at[other, k, c],
                    device_id=(o, v), device_id_type=MESH,
                ).wait_recv()
    for cond, finish in waits:
        pl.when(cond)(finish)

    @pl.when(v == owner)
    def _():
        for step in range(1, n_vir):
            far_strip(step).wait_send()

    keep.wait()
    again.wait()


def exchange(n_occ, n_vir, main, extra):
    pairs, cdim = main.shape
    ratio = n_vir // n_occ
    line = LINE if n_vir % LINE == 0 else 1
    wide = n_vir // line
    return pl.pallas_call(
        functools.partial(exchange_kernel, n_occ, n_vir),
        out_shape=(
            jax.ShapeDtypeStruct((n_vir + 1, pairs, cdim), jnp.bfloat16),
            jax.ShapeDtypeStruct((n_occ, ratio, pairs, cdim), jnp.bfloat16),
        ),
        in_specs=[pl.BlockSpec(memory_space=pl.ANY)] * 2,
        out_specs=(pl.BlockSpec(memory_space=pl.ANY),) * 2,
        scratch_shapes=[
            pltpu.SemaphoreType.DMA((3,)),
            pltpu.SemaphoreType.DMA((n_vir, CHUNKS + 1, wide + 1)),
            pltpu.SemaphoreType.DMA((n_vir, CHUNKS + 1)),
            pltpu.SemaphoreType.DMA((n_vir, CHUNKS)),
            pltpu.SemaphoreType.DMA((n_occ, ratio, CHUNKS)),
            pltpu.SemaphoreType.DMA((n_vir,)),
        ],
        compiler_params=pltpu.CompilerParams(collective_id=0, has_side_effects=True),
    )(main, extra)


def flip(block):
    a, b, cdim = block.shape
    return jnp.transpose(block.reshape(a, b, TILE, TILE), (1, 0, 3, 2)).reshape(b, a, cdim)


def add(a, b):
    return (a.astype(jnp.float32) + b.astype(jnp.float32)).astype(jnp.bfloat16)


def per_device(sizes, amplitudes, screen, integrals):
    n_occ, n_vir = sizes
    rows, cols, cdim = amplitudes.shape
    ratio = rows // cols
    assert ratio == 2 and n_vir == ratio * n_occ
    o, v = lax.axis_index("occ"), lax.axis_index("vir")
    q, r = v // ratio, lax.rem(v, ratio)

    def pick(o, q, r):
        return jnp.where(o < q, r, 1 - r)

    parts = (amplitudes * screen[:, :, None].astype(jnp.bfloat16)).reshape(ratio, cols, cols, cdim)

    def half(k):
        return jnp.where(k == 0, parts[0], parts[1])

    pairs = []
    for a in range(n_occ):
        for b in range(n_vir):
            c, s = divmod(b, ratio)
            t = s if c < a else 1 - s
            pairs.append((a * n_vir + b, c * n_vir + a * ratio + t))
    got = lax.ppermute(half(jnp.where(q < o, r, 1 - r)), ("occ", "vir"), pairs)
    mixed = add(half(pick(o, q, r)), flip(got))
    inner = add(half(r), flip(half(r)))
    main = jnp.where(o == q, inner, mixed)
    gathered, turned = exchange(n_occ, n_vir, main.reshape(cols * cols, cdim), mixed.reshape(cols * cols, cdim))

    width = integrals.shape[1]
    permuted = jnp.transpose(integrals.reshape(TILE, TILE, width), (1, 0, 2)).reshape(cdim, width)
    straight = jnp.dot(gathered.reshape(-1, cdim), integrals, preferred_element_type=jnp.float32)
    crossed = jnp.dot(turned.reshape(-1, cdim), permuted, preferred_element_type=jnp.float32)
    shape = (-1, cols, cols, width // SLAB_VIRT, SLAB_VIRT)
    straight = straight.astype(jnp.bfloat16).reshape(shape)
    crossed = jnp.swapaxes(crossed.astype(jnp.bfloat16).reshape(shape), 1, 2)
    blocks = jnp.concatenate([straight, crossed])
    k = jnp.arange(ratio)[:, None]
    w = jnp.arange(n_vir)[None, :]
    p, s = w // ratio, w % ratio
    first = n_vir + 1
    apart = jnp.where(pick(o, p, s) == k, w, first + p * ratio + k)
    same = jnp.where(k == s, w, jnp.where(k == 0, n_vir, first + o * ratio))
    index = jnp.where(p == o, same, apart)
    out = jnp.take(blocks, index, axis=0, mode="clip")
    return jnp.transpose(out, (0, 2, 1, 3, 4, 5)).reshape(rows, n_vir * cols, -1, SLAB_VIRT)


def solution(mesh):
    sizes = (mesh.shape["occ"], mesh.shape["vir"])
    return jax.shard_map(
        functools.partial(per_device, sizes),
        mesh=mesh,
        in_specs=(P("occ", "vir", None), P("occ", "vir"), P(None, "vir")),
        out_specs=P("occ", None, "vir", None),
        check_vma=False,
    )
```

time: 415 us -> 165 us (0.40); the launches traced: 410 us -> 165 us
  waiting for transfers between devices: 124 us -> 0.01 us
  blocking collectives: 101 us -> 0 us
  Pallas kernels: 0 us -> 80.6 us
  local copies, waits for them, and re-layouts: 115 us -> 47.1 us
  matrix products: 41.8 us -> 27.4 us
  between operations: 13.4 us -> 0.1 us
  other arithmetic: 15.1 us -> 7.98 us
    all_gather x1 -> x0, waiting for transfers between devices: 124 us -> none  [per_device(): whole = lax.all_gather(masked, 'vir', axis=1, tiled=True)]
    all_to_all x1 -> x0, blocking collectives: 101 us -> none  [per_device(): lax.all_to_all(whole, 'occ', split_axis=1, concat_axis=0, tiled=True)]
    convert_element_type x5 -> x7, local copies, waits for them, and re-layouts: 100 us -> 16.1 us  [the longest x6 16 us: add(): return (a.astype(jnp.float32) + b.astype(jnp.float32)).astype(jnp.bfloat16)]
    pallas_call x0 -> x1, Pallas kernels: none -> 80.6 us  [exchange(): pl.pallas_call(functools.partial(exchange_kernel, n_occ, n_vir), out_shap...]
    transpose x0 -> x1, local copies, waits for them, and re-layouts: none -> 18.6 us  [per_device(): jnp.transpose(integrals.reshape(TILE, TILE, width), (1, 0, 2))]
    dot_general x1 -> x2, matrix products: 41.8 us -> 27.4 us  [the longest x1 15 us: per_device(): jnp.dot(gathered.reshape(-1, cdim), integrals, preferred_element_type=jnp...]
    convert_element_type x2 -> x1, other arithmetic: 12.8 us -> 0.69 us  [per_device(): screen[:, :, None].astype(jnp.bfloat16)]
    all_gather x1 -> x0, local copies, waits for them, and re-layouts: 11.2 us -> none  [per_device(): whole = lax.all_gather(masked, 'vir', axis=1, tiled=True)]
  transfers between devices with their start and end apart: 1 -> 1, of which waited for: 1 -> 0; matrix products, arithmetic and copies ran while one was open for 0% -> 16% of each run, Pallas kernels for 0% -> 0%
where the time goes in v2:
time: 165 us
  Pallas kernels  80.6 us (49%)
  local copies, waits for them, and re-layouts  47.1 us (29%)
  matrix products  27.4 us (17%)
  other arithmetic  7.98 us (5%)
    pallas_call x1, Pallas kernels, exchange(): pl.pallas_call(functools.partial(exchange_kernel, n_occ, n_vir), out_shap...  80.6 us
    transpose x1, local copies, waits for them, and re-layouts, per_device(): jnp.transpose(integrals.reshape(TILE, TILE, width), (1, 0, 2))  18.6 us
    convert_element_type x6, local copies, waits for them, and re-layouts, add(): return (a.astype(jnp.float32) + b.astype(jnp.float32)).astype(jnp.bfloat16)  16 us
    dot_general x1, matrix products, per_device(): jnp.dot(gathered.reshape(-1, cdim), integrals, preferred_element_type=jnp...  15 us
    dot_general x1, matrix products, per_device(): jnp.dot(turned.reshape(-1, cdim), permuted, preferred_element_type=jnp.fl...  12.4 us
    gather x2, local copies, waits for them, and re-layouts, per_device(): out = jnp.take(blocks, index, axis=0, mode='clip')  11 us
  transfers between devices with their start and end apart: 1, of which 0 were waited for; matrix products, arithmetic and copies ran while one was open for 16% of the time, Pallas kernels for 0%

profile of v2, /device:TPU:24, one launch (start us, length us, event | category | flops | bytes accessed | tf_op | source)
XLA Modules:
  0.0 164.7 jit_solution(9788673916753297610)
XLA Ops:
  0.0 0.7 convert_element_type.46
  0.7 0.1 copy.14
  0.8 1.4 broadcast_multiply_fusion
  2.1 0.9 broadcast_select_fusion
  3.1 1.5 collective-permute-start
  4.6 0.1 fusion.2
  4.7 0.1 reshape.282
  4.8 2.2 %reshape.278 = f32[8,8,64,64]{3,2,1,0:T(8,128)} reshape(f32[8,8,4096]{2,1,0:T(8,128)S(1)} %get-tuple-element.12) | data formatting | bytes 2097152 | tf_op jit(solution)/shard_map/convert_element_type | solution.py:192
  7.0 2.9 %copy.15 = f32[8,8,64,64]{2,3,0,1:T(8,128)} copy(f32[8,8,64,64]{3,2,1,0:T(8,128)} %reshape.278) | data formatting | bytes 2097152 | tf_op jit(solution)/shard_map/convert_element_type | solution.py:192
  9.9 2.1 %reshape.276 = f32[8,8,4096]{2,1,0:T(8,128)S(1)} reshape(f32[8,8,64,64]{3,2,1,0:T(8,128)} %bitcast.35) | data formatting | bytes 2097152 | tf_op jit(solution)/shard_map/convert_element_type | solution.py:192
  12.0 18.6 %copy.17 = bf16[64,64,2048]{2,1,0:T(8,128)(2,1)} copy(bf16[64,64,2048]{2,0,1:T(8,128)(2,1)} %bitcast.30) | data formatting | bytes 33554432 | tf_op jit(solution)/shard_map/transpose | solution.py:224
  30.6 0.0 collective-permute-done
  30.7 3.0 %reshape.279 = f32[8,8,64,64]{3,2,1,0:T(8,128)} reshape(bf16[8,8,4096]{2,1,0:T(8,128)(2,1)} %collective-permute-done) | data formatting | bytes 1572864 | tf_op jit(solution)/shard_map/convert_element_type | solution.py:192
  33.7 2.9 %copy.16 = f32[8,8,64,64]{3,2,1,0:T(8,128)} copy(f32[8,8,64,64]{2,3,0,1:T(8,128)} %bitcast.34) | data formatting | bytes 2097152 | tf_op jit(solution)/shard_map/convert_element_type | solution.py:192
  36.6 2.9 %reshape.277 = f32[8,8,4096]{2,1,0:T(8,128)} reshape(f32[8,8,64,64]{3,2,1,0:T(8,128)} %copy.16) | data formatting | bytes 2097152 | tf_op jit(solution)/shard_map/convert_element_type | solution.py:192
  39.5 2.5 %fusion.1 = (bf16[64,4096]{1,0:T(8,128)(2,1)}, bf16[8,8,4096]{2,1,0:T(8,128)(2,1)}) fusion(f32[8,8,4096]{2,1,0:T(8,128)S(1)} %get-tuple-element.12, f32[8,8,4096]{2,1,0:T(8,128)S(1)} %reshape.276, pred[]{:T(512)S(6)} %eq.76, f32[8,8,4096]{2,1,0:T(8,128)} %reshape.277, bf16[16,8,4096]{2,1,0:T(8,128)(2,1)S(1)} %broadcast_multiply_fusion, pred[]{:T(512)S(6)} %eq.78), kind=kLoop, calls=%fused_computation.8 | loop fusion | flops 1835008 | bytes 5242882 | tf_op jit(solution)/shard_map/reshape | solution.py:221
  42.0 80.6 %shard_map.37 = (bf16[9,64,4096]{2,1,0:T(8,128)(2,1)}, bf16[4,2,64,4096]{3,2,1,0:T(8,128)(2,1)}) custom-call(bf16[64,4096]{1,0:T(8,128)(2,1)} %get-tuple-element.9.main, bf16[64,4096]{1,0:T(8,128)(2,1)} %bitcast.38), custom_call_target="tpu_custom_call" | custom-call | tf_op jit(solution)/shard_map/pallas_call | solution.py:166
  122.6 0.0 copy-start
  122.6 15.0 %convolution_convert_fusion = bf16[576,2048]{1,0:T(8,128)(2,1)S(1)} fusion(bf16[576,4096]{1,0:T(8,128)(2,1)} %bitcast.39, bf16[4096,2048]{1,0:T(8,128)(2,1)} %param.5), kind=kOutput, calls=%fused_computation.2 | convolution fusion | flops 9664856064 | bytes 23855104 | tf_op jit(solution)/shard_map/dot_general | solution.py:225
  137.6 0.0 copy-done
  137.6 12.4 %convolution_convert_fusion.1 = bf16[512,2048]{1,0:T(8,128)(2,1)S(1)} fusion(bf16[512,4096]{1,0:T(8,128)(2,1)S(1)} %bitcast.40, bf16[4096,2048]{1,0:T(8,128)(2,1)} %bitcast.31), kind=kOutput, calls=%fused_computation.3 | convolution fusion | flops 8590983168 | bytes 23068672 | tf_op jit(solution)/shard_map/dot_general | solution.py:226
  150.0 1.4 copy.21
  151.4 2.4 %pad_maximum_fusion = bf16[17,8,8,16,128]{4,2,3,1,0:T(8,128)(2,1)} fusion(bf16[8,8,8,16,128]{4,2,3,1,0:T(8,128)(2,1)S(1)} %bitcast.33, bf16[9,8,8,16,128]{4,2,3,1,0:T(8,128)(2,1)S(1)} %bitcast.36), kind=kLoop, calls=%fused_computation.1 | loop fusion | flops 2228224 | bytes 8912896 | tf_op jit(solution)/shard_map/concatenate | solution.py:230
  153.8 5.3 %gather_fusion = bf16[16,8,8,16,128]{4,2,3,1,0:T(8,128)(2,1)} fusion(bf16[17,8,8,16,128]{4,2,3,1,0:T(8,128)(2,1)} %pad_maximum_fusion, s32[1024]{0:T(1024)S(1)} %pad_clamp_fusion), kind=kCustom, calls=%fused_computation | custom fusion | bytes 8388672 | tf_op jit(solution)/shard_map/jit(_take)/gather | solution.py:238
  159.1 5.6 %copy.19 = bf16[2,8,8,8,16,128]{5,4,3,1,2,0:T(8,128)(2,1)} copy(bf16[2,8,8,8,16,128]{5,3,4,2,1,0:T(8,128)(2,1)} %bitcast.32) | data formatting | bytes 8388608 | tf_op jit(solution)/shard_map/jit(_take)/gather | solution.py:238
  (5 shorter events, 0.0 us)
Async XLA Ops:
  3.1 27.6 %collective-permute-start = (bf16[8,8,4096]{2,1,0:T(8,128)(2,1)}, bf16[8,8,4096]{2,1,0:T(8,128)(2,1)}, u32[]{:S(2)}, u32[]{:S(2)}) collective-permute-start(bf16[8,8,4096]{2,1,0:T(8,128)(2,1)} %get-tuple-element.11), channel_id=1, source_target_pairs={{0,1},{1,0},{2,9},{3,8},{4,17},{5,16},{6,25},{7,24},{8,2},{9,3},{1... | collective-permute-start | bytes 1572872 | tf_op jit(solution)/shard_map/ppermute | solution.py:217
  122.6 15.0 %copy-start = (bf16[4,2,64,4096]{3,2,1,0:T(8,128)(2,1)S(1)}, bf16[4,2,64,4096]{3,2,1,0:T(8,128)(2,1)}, u32[]{:S(2)}) copy-start(bf16[4,2,64,4096]{3,2,1,0:T(8,128)(2,1)} %get-tuple-element.8) | copy-start | bytes 12582916

commit v3 on v2

--- a/solution.py
+++ b/solution.py
@@ -1,4 +1,5 @@
 import functools
+import math
 
 import jax
 import jax.numpy as jnp
@@ -11,10 +12,23 @@
 SLAB_VIRT = 128
 LINE = 4
 CHUNKS = 2
+STEP = 16
+WIDE = 512
+NARROW = 256
 MESH = pl.DeviceIdType.MESH
 
 
-def exchange_kernel(n_occ, n_vir, main, extra, gathered, turned, local_sem, send_sem, recv_sem, turn_send, turn_recv, extra_send):
+def pair_swap(n):
+    to = lax.broadcasted_iota(jnp.int32, (n * n, n * n), 0)
+    at = lax.broadcasted_iota(jnp.int32, (n * n, n * n), 1)
+    hit = (lax.rem(to, n) == at // n) & (to // n == lax.rem(at, n))
+    return jnp.where(hit, 1.0, 0.0).astype(jnp.bfloat16)
+
+
+def exchange_kernel(
+    n_occ, n_vir, main, extra, slab, out, gathered, turned, straight, crossed,
+    local_sem, send_sem, recv_sem, turn_send, turn_recv, extra_send,
+):
     ratio = n_vir // n_occ
     line = LINE if n_vir % LINE == 0 else 1
     wide = n_vir // line
@@ -24,6 +38,10 @@
     piece = pairs // CHUNKS
     strip = cdim // n_vir
     owner = o * ratio + 1
+    cols = out.shape[2]
+    width = out.shape[3]
+    load = pltpu.make_async_copy(slab, straight, local_sem.at[0])
+    load.start()
 
     barrier = pltpu.get_barrier_semaphore()
     for step in range(1, n_vir):
@@ -89,7 +107,41 @@
         spread(cond, source, c, False, up, down, sides)
 
     always = v >= 0
-    keep = pltpu.make_async_copy(main, gathered.at[v], local_sem.at[0])
+
+    def permute(part, count):
+        swap = pair_swap(STEP)
+        across_c = TILE // STEP
+
+        @pl.loop(part * across_c**2 // count, (part + 1) * across_c**2 // count)
+        def _(at):
+            c = pl.ds(pl.multiple_of(at // across_c * STEP, STEP), STEP)
+            d = pl.ds(pl.multiple_of(lax.rem(at, across_c) * STEP, STEP), STEP)
+            for n in range(width // WIDE):
+                lanes = pl.ds(n * WIDE, WIDE)
+                block = straight[c, d, lanes].reshape(STEP * STEP, WIDE)
+                moved = jnp.dot(swap, block, preferred_element_type=jnp.float32)
+                crossed[d, c, lanes] = moved.astype(jnp.bfloat16).reshape(STEP, STEP, WIDE)
+
+    def multiply(left, weights, places):
+        @pl.loop(0, width // NARROW)
+        def _(n):
+            lanes = pl.ds(pl.multiple_of(n * NARROW, NARROW), NARROW)
+            right = weights[:, :, lanes].reshape(cdim, NARROW)
+            got = jnp.dot(left(), right, preferred_element_type=jnp.float32)
+            for at, (k, source) in enumerate(places):
+                rows = got[at * pairs : (at + 1) * pairs].reshape(cols, cols, NARROW)
+                out[pl.ds(k * cols, cols), source, :, lanes] = rows.astype(jnp.bfloat16)
+
+    def row_of(occ, vir):
+        q, r = vir // ratio, lax.rem(vir, ratio)
+        return jnp.where(occ <= q, r, 1 - r)
+
+    def group(zz):
+        sources = [zz * wide + step for step in range(wide)]
+        multiply(
+            lambda: gathered[pl.ds(zz * wide, wide)].reshape(wide * pairs, cdim),
+            straight, [(row_of(o, w), w) for w in sources],
+        )
 
     def strip_of(target):
         return extra.at[:, pl.ds(pl.multiple_of(target * strip, strip), strip)]
@@ -114,7 +166,7 @@
             far_strip(step).start()
         own_strip.wait()
 
-    keep.start()
+    gathered[v] = main[...]
 
     @pl.when(v != owner)
     def _():
@@ -133,9 +185,20 @@
                 arrive(z >= e, (z - e) * wide + side, c, False, False, False)
                 if e:
                     arrive(z < line - e, (z + e) * wide + side, c, False, False, False)
-
-    again = pltpu.make_async_copy(gathered.at[n_vir], turned.at[o, 0], local_sem.at[2])
-    again.start()
+            if d <= 2 and c < CHUNKS:
+                if d == 1 and c == 0:
+                    load.wait()
+                permute((d - 1) * CHUNKS + c, 2 * CHUNKS)
+        if d == 1:
+            group(z)
+        else:
+            pl.when(z >= d - 1)(lambda: group(z - d + 1))
+            pl.when(z < line - d + 1)(lambda: group(z + d - 1))
+
+    multiply(lambda: gathered[n_vir], straight, [(0, owner)])
+    turned[o, 0] = gathered[n_vir]
+    for k in range(1, ratio):
+        turned[o, k] = gathered[n_vir]
     for step in range(1, n_occ):
         other = lax.rem(o + step, n_occ)
         for k in range(ratio):
@@ -146,6 +209,20 @@
                     send_sem=turn_send.at[0, c], recv_sem=turn_recv.at[other, k, c],
                     device_id=(o, v), device_id_type=MESH,
                 ).wait_recv()
+    swap = pair_swap(cols)
+
+    @pl.loop(0, n_occ * ratio)
+    def _(at):
+        p, k = at // ratio, lax.rem(at, ratio)
+        moved = jnp.dot(swap, turned[p, k], preferred_element_type=jnp.float32)
+        turned[p, k] = moved.astype(jnp.bfloat16)
+
+    places = []
+    for p in range(n_occ):
+        for k in range(ratio):
+            s = jnp.where(p < o, k, 1 - k)
+            places.append((jnp.where(p == o, 1, k), p * ratio + jnp.where(p == o, 0, s)))
+    multiply(lambda: turned[...].reshape(n_occ * ratio * pairs, cdim), crossed, places)
     for cond, finish in waits:
         pl.when(cond)(finish)
 
@@ -154,33 +231,35 @@
         for step in range(1, n_vir):
             far_strip(step).wait_send()
 
-    keep.wait()
-    again.wait()
-
-
-def exchange(n_occ, n_vir, main, extra):
+
+def ladder(n_occ, n_vir, main, extra, slab):
     pairs, cdim = main.shape
     ratio = n_vir // n_occ
     line = LINE if n_vir % LINE == 0 else 1
     wide = n_vir // line
+    cols = math.isqrt(pairs)
     return pl.pallas_call(
         functools.partial(exchange_kernel, n_occ, n_vir),
-        out_shape=(
-            jax.ShapeDtypeStruct((n_vir + 1, pairs, cdim), jnp.bfloat16),
-            jax.ShapeDtypeStruct((n_occ, ratio, pairs, cdim), jnp.bfloat16),
-        ),
-        in_specs=[pl.BlockSpec(memory_space=pl.ANY)] * 2,
-        out_specs=(pl.BlockSpec(memory_space=pl.ANY),) * 2,
+        out_shape=jax.ShapeDtypeStruct((ratio * cols, n_vir, cols, slab.shape[2]), jnp.bfloat16),
+        in_specs=[pl.BlockSpec(memory_space=pltpu.VMEM)] * 2 + [pl.BlockSpec(memory_space=pl.ANY)],
+        out_specs=pl.BlockSpec(memory_space=pltpu.VMEM),
         scratch_shapes=[
-            pltpu.SemaphoreType.DMA((3,)),
+            pltpu.VMEM((n_vir + 1, pairs, cdim), jnp.bfloat16),
+            pltpu.VMEM((n_occ, ratio, pairs, cdim), jnp.bfloat16),
+            pltpu.VMEM(slab.shape, jnp.bfloat16),
+            pltpu.VMEM(slab.shape, jnp.bfloat16),
+            pltpu.SemaphoreType.DMA((2,)),
             pltpu.SemaphoreType.DMA((n_vir, CHUNKS + 1, wide + 1)),
             pltpu.SemaphoreType.DMA((n_vir, CHUNKS + 1)),
             pltpu.SemaphoreType.DMA((n_vir, CHUNKS)),
             pltpu.SemaphoreType.DMA((n_occ, ratio, CHUNKS)),
             pltpu.SemaphoreType.DMA((n_vir,)),
         ],
-        compiler_params=pltpu.CompilerParams(collective_id=0, has_side_effects=True),
-    )(main, extra)
+        compiler_params=pltpu.CompilerParams(
+            collective_id=0, has_side_effects=True, vmem_limit_bytes=60 * 2**20
+        ),
+        cost_estimate=pl.CostEstimate(flops=2**35, bytes_accessed=2**25, transcendentals=0),
+    )(main, extra, slab)
 
 
 def flip(block):
@@ -218,25 +297,12 @@
     mixed = add(half(pick(o, q, r)), flip(got))
     inner = add(half(r), flip(half(r)))
     main = jnp.where(o == q, inner, mixed)
-    gathered, turned = exchange(n_occ, n_vir, main.reshape(cols * cols, cdim), mixed.reshape(cols * cols, cdim))
-
     width = integrals.shape[1]
-    permuted = jnp.transpose(integrals.reshape(TILE, TILE, width), (1, 0, 2)).reshape(cdim, width)
-    straight = jnp.dot(gathered.reshape(-1, cdim), integrals, preferred_element_type=jnp.float32)
-    crossed = jnp.dot(turned.reshape(-1, cdim), permuted, preferred_element_type=jnp.float32)
-    shape = (-1, cols, cols, width // SLAB_VIRT, SLAB_VIRT)
-    straight = straight.astype(jnp.bfloat16).reshape(shape)
-    crossed = jnp.swapaxes(crossed.astype(jnp.bfloat16).reshape(shape), 1, 2)
-    blocks = jnp.concatenate([straight, crossed])
-    k = jnp.arange(ratio)[:, None]
-    w = jnp.arange(n_vir)[None, :]
-    p, s = w // ratio, w % ratio
-    first = n_vir + 1
-    apart = jnp.where(pick(o, p, s) == k, w, first + p * ratio + k)
-    same = jnp.where(k == s, w, jnp.where(k == 0, n_vir, first + o * ratio))
-    index = jnp.where(p == o, same, apart)
-    out = jnp.take(blocks, index, axis=0, mode="clip")
-    return jnp.transpose(out, (0, 2, 1, 3, 4, 5)).reshape(rows, n_vir * cols, -1, SLAB_VIRT)
+    out = ladder(
+        n_occ, n_vir, main.reshape(cols * cols, cdim), mixed.reshape(cols * cols, cdim),
+        integrals.reshape(TILE, TILE, width),
+    )
+    return out.reshape(rows, n_vir * cols, -1, SLAB_VIRT)
 
 
 def solution(mesh):

time: 165 us -> 137 us (0.83)
  matrix products: 27.4 us -> 0 us
  local copies, waits for them, and re-layouts: 47.1 us -> 21.7 us
  Pallas kernels: 80.6 us -> 98.4 us
  waiting for transfers between devices: 0.01 us -> 8.13 us
  other arithmetic: 7.98 us -> 5.4 us
    dot_general x2 -> x0, matrix products: 27.4 us -> none  [the longest x1 15 us: per_device(): jnp.dot(gathered.reshape(-1, cdim), integrals, preferred_element_type=jnp...]
    transpose x1 -> x0, local copies, waits for them, and re-layouts: 18.6 us -> none  [per_device(): jnp.transpose(integrals.reshape(TILE, TILE, width), (1, 0, 2))]
    pallas_call x1, Pallas kernels: 80.6 us -> 98.4 us  [ladder(): pl.pallas_call(functools.partial(exchange_kernel, n_occ, n_vir), out_shap...]
    gather x2 -> x0, local copies, waits for them, and re-layouts: 11 us -> none  [per_device(): out = jnp.take(blocks, index, axis=0, mode='clip')]
    ppermute x1, waiting for transfers between devices: 0.01 us -> 8.13 us  [per_device(): got = lax.ppermute(half(jnp.where(q < o, r, 1 - r)), ('occ', 'vir'), pairs)]
    unnamed x2 -> x1, local copies, waits for them, and re-layouts: 0.01 us -> 5.62 us
    concatenate x1 -> x0, other arithmetic: 2.41 us -> none  [per_device(): blocks = jnp.concatenate([straight, crossed])]
  transfers between devices with their start and end apart: 1 -> 1, of which waited for: 0 -> 1; matrix products, arithmetic and copies ran while one was open for 16% -> 5% of each run, Pallas kernels for 0% -> 0%
where the time goes in v3:
time: 137 us; the launch traced here: 135 us
  Pallas kernels  98.4 us (72%)
  local copies, waits for them, and re-layouts  21.7 us (16%)
  waiting for transfers between devices  8.13 us (6%)
  other arithmetic  5.4 us (4%)
  starting transfers between devices  1.54 us (1%)
    pallas_call x1, Pallas kernels, ladder(): pl.pallas_call(functools.partial(exchange_kernel, n_occ, n_vir), out_shap...  98.4 us
    convert_element_type x6, local copies, waits for them, and re-layouts, add(): return (a.astype(jnp.float32) + b.astype(jnp.float32)).astype(jnp.bfloat16)  16 us
    ppermute x1, waiting for transfers between devices, per_device(): got = lax.ppermute(half(jnp.where(q < o, r, 1 - r)), ('occ', 'vir'), pairs)  8.13 us
    unnamed x1, local copies, waits for them, and re-layouts  5.62 us
  transfers between devices with their start and end apart: 1, of which 1 were waited for; matrix products, arithmetic and copies ran while one was open for 5% of the time, Pallas kernels for 0%

profile of v3, /device:TPU:24, one launch (start us, length us, event | category | flops | bytes accessed | tf_op | source)
XLA Modules:
  0.0 135.2 jit_solution(15946409345546547969)
XLA Ops:
  0.0 0.7 convert_element_type.40
  0.7 0.1 copy.4
  0.8 1.4 %broadcast_multiply_fusion = bf16[16,8,4096]{2,1,0:T(8,128)(2,1)S(1)} fusion(bf16[16,8,4096]{2,1,0:T(8,128)(2,1)} %param.3, bf16[16,8]{1,0:T(8,128)(2,1)S(1)} %copy.4), kind=kLoop, calls=%fused_computation.5 | loop fusion | flops 524288 | bytes 2097408 | tf_op jit(solution)/shard_map/mul | solution.py:285
  2.1 0.9 broadcast_select_fusion
  3.0 1.5 %collective-permute-start = (bf16[8,8,4096]{2,1,0:T(8,128)(2,1)}, bf16[8,8,4096]{2,1,0:T(8,128)(2,1)}, u32[]{:S(2)}, u32[]{:S(2)}) collective-permute-start(bf16[8,8,4096]{2,1,0:T(8,128)(2,1)} %get-tuple-element.7), channel_id=1, source_target_pairs={{0,1},{1,0},{2,9},{3,8},{4,17},{5,16},{6,25},{7,24},{8,2},{9,3},{1... | collective-permute-start | bytes 1572872 | tf_op jit(solution)/shard_map/ppermute | solution.py:296
  4.6 2.2 %reshape.37 = f32[8,8,64,64]{3,2,1,0:T(8,128)} reshape(f32[8,8,4096]{2,1,0:T(8,128)S(1)} %get-tuple-element.8) | data formatting | bytes 2097152 | tf_op jit(solution)/shard_map/convert_element_type | solution.py:271
  6.7 2.9 %copy.5 = f32[8,8,64,64]{2,3,0,1:T(8,128)} copy(f32[8,8,64,64]{3,2,1,0:T(8,128)} %reshape.37) | data formatting | bytes 2097152 | tf_op jit(solution)/shard_map/convert_element_type | solution.py:271
  9.7 2.1 %reshape.35 = f32[8,8,4096]{2,1,0:T(8,128)S(1)} reshape(f32[8,8,64,64]{3,2,1,0:T(8,128)} %bitcast.16) | data formatting | bytes 2097152 | tf_op jit(solution)/shard_map/convert_element_type | solution.py:271
  11.8 8.1 %collective-permute-done = bf16[8,8,4096]{2,1,0:T(8,128)(2,1)} collective-permute-done((bf16[8,8,4096]{2,1,0:T(8,128)(2,1)}, bf16[8,8,4096]{2,1,0:T(8,128)(2,1)}, u32[]{:S(2)}, u32[]{:S(2)}) %collective-permute-start) | collective-permute-done | bytes 524320 | tf_op jit(solution)/shard_map/ppermute | solution.py:296
  19.9 3.0 %reshape.38 = f32[8,8,64,64]{3,2,1,0:T(8,128)} reshape(bf16[8,8,4096]{2,1,0:T(8,128)(2,1)} %collective-permute-done) | data formatting | bytes 1572864 | tf_op jit(solution)/shard_map/convert_element_type | solution.py:271
  22.9 2.9 %copy.6 = f32[8,8,64,64]{3,2,1,0:T(8,128)} copy(f32[8,8,64,64]{2,3,0,1:T(8,128)} %bitcast.15) | data formatting | bytes 2097152 | tf_op jit(solution)/shard_map/convert_element_type | solution.py:271
  25.9 2.9 %reshape.36 = f32[8,8,4096]{2,1,0:T(8,128)} reshape(f32[8,8,64,64]{3,2,1,0:T(8,128)} %copy.6) | data formatting | bytes 2097152 | tf_op jit(solution)/shard_map/convert_element_type | solution.py:271
  28.8 2.5 %fusion.1 = (bf16[64,4096]{1,0:T(8,128)(2,1)}, bf16[8,8,4096]{2,1,0:T(8,128)(2,1)}) fusion(f32[8,8,4096]{2,1,0:T(8,128)S(1)} %get-tuple-element.8, f32[8,8,4096]{2,1,0:T(8,128)S(1)} %reshape.35, pred[]{:T(512)S(6)} %eq.13, f32[8,8,4096]{2,1,0:T(8,128)} %reshape.36, bf16[16,8,4096]{2,1,0:T(8,128)(2,1)S(1)} %broadcast_multiply_fusion, pred[]{:T(512)S(6)} %eq.15), kind=kLoop, calls=%fused_computation.3 | loop fusion | flops 1835008 | bytes 5242882 | tf_op jit(solution)/shard_map/reshape | solution.py:302
  31.2 98.4 %shard_map.37 = bf16[16,8,8,2048]{3,2,1,0:T(8,128)(2,1)} custom-call(bf16[64,4096]{1,0:T(8,128)(2,1)} %get-tuple-element.5.main, bf16[64,4096]{1,0:T(8,128)(2,1)} %bitcast.18, bf16[64,64,2048]{2,1,0:T(8,128)(2,1)} %bitcast.19), custom_call_target="tpu_custom_call" | custom-call | flops 34359738368 | bytes 33554432 | tf_op jit(solution)/shard_map/pallas_call | solution.py:241
  129.6 5.6 %copy.7 = bf16[128,8,16,128]{3,2,1,0:T(8,128)(2,1)} copy(bf16[128,8,16,128]{3,1,2,0:T(8,128)(2,1)} %bitcast.17) | data formatting | bytes 8388608
Async XLA Ops:
  3.0 16.9 %collective-permute-start = (bf16[8,8,4096]{2,1,0:T(8,128)(2,1)}, bf16[8,8,4096]{2,1,0:T(8,128)(2,1)}, u32[]{:S(2)}, u32[]{:S(2)}) collective-permute-start(bf16[8,8,4096]{2,1,0:T(8,128)(2,1)} %get-tuple-element.7), channel_id=1, source_target_pairs={{0,1},{1,0},{2,9},{3,8},{4,17},{5,16},{6,25},{7,24},{8,2},{9,3},{1... | collective-permute-start | bytes 1572872 | tf_op jit(solution)/shard_map/ppermute | solution.py:296

commit v4 on v3

--- a/solution.py
+++ b/solution.py
@@ -11,7 +11,8 @@
 TILE = 64
 SLAB_VIRT = 128
 LINE = 4
-CHUNKS = 2
+CHUNKS = 4
+PIECES = 2
 STEP = 16
 WIDE = 512
 NARROW = 256
@@ -293,8 +294,14 @@
             c, s = divmod(b, ratio)
             t = s if c < a else 1 - s
             pairs.append((a * n_vir + b, c * n_vir + a * ratio + t))
-    got = lax.ppermute(half(jnp.where(q < o, r, 1 - r)), ("occ", "vir"), pairs)
-    mixed = add(half(pick(o, q, r)), flip(got))
+    sent = half(jnp.where(q < o, r, 1 - r))
+    kept = half(pick(o, q, r))
+    cut = cols // PIECES
+    sums = []
+    for at in range(0, cols, cut):
+        got = lax.ppermute(sent[:, at : at + cut], ("occ", "vir"), pairs)
+        sums.append(add(kept[at : at + cut], flip(got)))
+    mixed = jnp.concatenate(sums)
     inner = add(half(r), flip(half(r)))
     main = jnp.where(o == q, inner, mixed)
     width = integrals.shape[1]

time: 137 us -> 135 us (0.985)
  waiting for transfers between devices: 8.13 us -> 2.76 us
  starting transfers between devices: 1.54 us -> 5.37 us
  local copies, waits for them, and re-layouts: 21.7 us -> 20 us
    ppermute x1 -> x2, waiting for transfers between devices: 8.13 us -> 2.76 us  [per_device(): got = lax.ppermute(sent[:, at:at + cut], ('occ', 'vir'), pairs)]
    convert_element_type x6 -> x9, local copies, waits for them, and re-layouts: 16 us -> 12 us  [add(): return (a.astype(jnp.float32) + b.astype(jnp.float32)).astype(jnp.bfloat16)]
    ppermute x1 -> x2, starting transfers between devices: 1.54 us -> 5.37 us  [per_device(): got = lax.ppermute(sent[:, at:at + cut], ('occ', 'vir'), pairs)]
    reshape x1 -> x0, other arithmetic: 2.46 us -> none  [per_device(): main.reshape(cols * cols, cdim)]
    convert_element_type x0 -> x1, other arithmetic: none -> 1.66 us  [add(): return (a.astype(jnp.float32) + b.astype(jnp.float32)).astype(jnp.bfloat16)]
    reshape x0 -> x1, local copies, waits for them, and re-layouts: none -> 1.55 us  [per_device(): mixed.reshape(cols * cols, cdim)]
    unnamed x1 -> x3, local copies, waits for them, and re-layouts: 5.62 us -> 5.62 us
  transfers between devices with their start and end apart: 1 -> 2, of which waited for: 1 -> 2; matrix products, arithmetic and copies ran while one was open for 5% -> 6% of each run, Pallas kernels for 0% -> 0%
where the time goes in v4:
time: 135 us; the launch traced here: 134 us
  Pallas kernels  99.5 us (74%)
  local copies, waits for them, and re-layouts  20 us (15%)
  other arithmetic  6.09 us (5%)
  starting transfers between devices  5.37 us (4%)
  waiting for transfers between devices  2.76 us (2%)
    pallas_call x1, Pallas kernels, ladder(): pl.pallas_call(functools.partial(exchange_kernel, n_occ, n_vir), out_shap...  99.5 us
    convert_element_type x9, local copies, waits for them, and re-layouts, add(): return (a.astype(jnp.float32) + b.astype(jnp.float32)).astype(jnp.bfloat16)  12 us
    unnamed x3, local copies, waits for them, and re-layouts  5.62 us
    ppermute x2, starting transfers between devices, per_device(): got = lax.ppermute(sent[:, at:at + cut], ('occ', 'vir'), pairs)  5.37 us
    ppermute x2, waiting for transfers between devices, per_device(): got = lax.ppermute(sent[:, at:at + cut], ('occ', 'vir'), pairs)  2.76 us
  transfers between devices with their start and end apart: 2, of which 2 were waited for; matrix products, arithmetic and copies ran while one was open for 6% of the time, Pallas kernels for 0%

profile of v4, /device:TPU:24, one launch (start us, length us, event | category | flops | bytes accessed | tf_op | source)
XLA Modules:
  0.0 133.8 jit_solution(14614132358351114626)
XLA Ops:
  0.0 0.7 convert_element_type.58
  0.7 2.4 %copy_multiply_fusion = bf16[16,8,4096]{2,0,1:T(8,128)(2,1)S(1)} fusion(bf16[16,8,4096]{2,1,0:T(8,128)(2,1)} %param.3, bf16[16,8]{0,1:T(8,128)(2,1)S(1)} %convert_element_type.58), kind=kLoop, calls=%fused_computation | loop fusion | flops 524288 | bytes 2097408 | tf_op jit(solution)/shard_map/mul | solution.py:286
  3.1 1.0 broadcast_select_fusion.1
  4.0 0.8 fusion.1
  4.8 1.5 %collective-permute-start.1 = (bf16[8,4,4096]{2,0,1:T(8,128)(2,1)}, bf16[8,4,4096]{2,0,1:T(8,128)(2,1)}, u32[]{:S(2)}, u32[]{:S(2)}) collective-permute-start(bf16[8,4,4096]{2,0,1:T(8,128)(2,1)} %get-tuple-element.13), channel_id=1, source_target_pairs={{0,1},{1,0},{2,9},{3,8},{4,17},{5,16},{6,25},{7,24},{8,2},{9,3},{1... | collective-permute-start | bytes 786440 | tf_op jit(solution)/shard_map/ppermute | solution.py:302
  6.4 3.8 %collective-permute-start = (bf16[8,4,4096]{2,0,1:T(8,128)(2,1)}, bf16[8,4,4096]{2,0,1:T(8,128)(2,1)S(1)}, u32[]{:S(2)}, u32[]{:S(2)}) collective-permute-start(bf16[8,4,4096]{2,0,1:T(8,128)(2,1)} %get-tuple-element.12), channel_id=1, source_target_pairs={{0,1},{1,0},{2,9},{3,8},{4,17},{5,16},{6,25},{7,24},{8,2},{9,3},{1... | collective-permute-start | bytes 786440 | tf_op jit(solution)/shard_map/ppermute | solution.py:302
  10.2 2.2 %reshape.44 = f32[8,8,64,64]{3,2,0,1:T(8,128)} reshape(f32[8,8,4096]{2,0,1:T(8,128)S(1)} %get-tuple-element.7) | data formatting | bytes 2097152 | tf_op jit(solution)/shard_map/convert_element_type | solution.py:272
  12.4 1.9 %copy.19 = f32[8,8,64,64]{2,3,1,0:T(8,128)S(1)} copy(f32[8,8,64,64]{3,2,0,1:T(8,128)} %reshape.44) | data formatting | bytes 2097152 | tf_op jit(solution)/shard_map/convert_element_type | solution.py:272
  14.3 1.6 %reshape.41 = f32[8,8,4096]{2,0,1:T(8,128)} reshape(f32[8,8,64,64]{3,2,0,1:T(8,128)S(1)} %bitcast.31) | data formatting | bytes 2097152 | tf_op jit(solution)/shard_map/convert_element_type | solution.py:272
  15.9 0.6 collective-permute-done.1
  16.5 1.4 %reshape.46 = f32[8,4,64,64]{3,2,0,1:T(8,128)S(1)} reshape(bf16[8,4,4096]{2,0,1:T(8,128)(2,1)} %collective-permute-done.1) | data formatting | bytes 786432 | tf_op jit(solution)/shard_map/convert_element_type | solution.py:272
  17.8 0.3 copy.27
  18.2 0.0 copy-start
  18.2 1.2 reshape.48
  19.4 2.2 %collective-permute-done = bf16[8,4,4096]{2,0,1:T(8,128)(2,1)S(1)} collective-permute-done((bf16[8,4,4096]{2,0,1:T(8,128)(2,1)}, bf16[8,4,4096]{2,0,1:T(8,128)(2,1)S(1)}, u32[]{:S(2)}, u32[]{:S(2)}) %collective-permute-start) | collective-permute-done | bytes 262176 | tf_op jit(solution)/shard_map/ppermute | solution.py:302
  21.6 0.4 reshape.45
  22.0 1.3 copy.26
  23.4 1.7 %reshape.47 = f32[4,8,4096]{2,0,1:T(4,128)S(1)} reshape(f32[4,8,64,64]{3,2,0,1:T(8,128)} %copy.26) | data formatting | bytes 1048576 | tf_op jit(solution)/shard_map/convert_element_type | solution.py:272
  25.0 1.7 %add_convert_fusion.2 = (bf16[4,8,4096]{2,0,1:T(4,128)(2,1)S(1)}, bf16[4,8,4096]{2,0,1:T(4,128)(2,1)S(1)}) fusion(f32[4,8,4096]{2,0,1:T(4,128)S(1)} %reshape.47, bf16[8,8,4096]{2,0,1:T(8,128)(2,1)} %get-tuple-element.5, f32[4,8,4096]{2,0,1:T(4,128)} %reshape.48), kind=kLoop, calls=%fused_computation.7 | loop fusion | flops 786432 | bytes 2097152 | tf_op jit(solution)/shard_map/convert_element_type | solution.py:272
  26.7 0.0 copy-done
  26.7 0.4 pad_maximum_fusion
  27.1 1.6 %copy_bitcast_fusion = (bf16[64,4096]{1,0:T(8,128)(2,1)}, bf16[64,4096]{1,0:T(8,128)(2,1)}) fusion(bf16[8,8,4096]{2,0,1:T(8,128)(2,1)S(1)} %get-tuple-element.8, bf16[8,8,4096]{2,0,1:T(8,128)(2,1)S(1)} %get-tuple-element.9), kind=kLoop, calls=%fused_computation.4 | loop fusion | bytes 2097152 | tf_op jit(solution)/shard_map/reshape | solution.py:309
  28.7 99.5 %shard_map.37 = bf16[16,8,8,2048]{3,2,1,0:T(8,128)(2,1)} custom-call(bf16[64,4096]{1,0:T(8,128)(2,1)} %get-tuple-element.15.main, bf16[64,4096]{1,0:T(8,128)(2,1)} %get-tuple-element.14.extra, bf16[64,64,2048]{2,1,0:T(8,128)(2,1)} %bitcast.35), custom_call_target="tpu_custom_call" | custom-call | flops 34359738368 | bytes 33554432 | tf_op jit(solution)/shard_map/pallas_call | solution.py:242
  128.2 5.6 %copy.30 = bf16[128,8,16,128]{3,2,1,0:T(8,128)(2,1)} copy(bf16[128,8,16,128]{3,1,2,0:T(8,128)(2,1)} %bitcast.34) | data formatting | bytes 8388608
Async XLA Ops:
  4.8 11.6 %collective-permute-start.1 = (bf16[8,4,4096]{2,0,1:T(8,128)(2,1)}, bf16[8,4,4096]{2,0,1:T(8,128)(2,1)}, u32[]{:S(2)}, u32[]{:S(2)}) collective-permute-start(bf16[8,4,4096]{2,0,1:T(8,128)(2,1)} %get-tuple-element.13), channel_id=1, source_target_pairs={{0,1},{1,0},{2,9},{3,8},{4,17},{5,16},{6,25},{7,24},{8,2},{9,3},{1... | collective-permute-start | bytes 786440 | tf_op jit(solution)/shard_map/ppermute | solution.py:302
  6.4 15.3 %collective-permute-start = (bf16[8,4,4096]{2,0,1:T(8,128)(2,1)}, bf16[8,4,4096]{2,0,1:T(8,128)(2,1)S(1)}, u32[]{:S(2)}, u32[]{:S(2)}) collective-permute-start(bf16[8,4,4096]{2,0,1:T(8,128)(2,1)} %get-tuple-element.12), channel_id=1, source_target_pairs={{0,1},{1,0},{2,9},{3,8},{4,17},{5,16},{6,25},{7,24},{8,2},{9,3},{1... | collective-permute-start | bytes 786440 | tf_op jit(solution)/shard_map/ppermute | solution.py:302
  18.2 8.5 %copy-start = (f32[8,8,4096]{2,0,1:T(8,128)S(1)}, f32[8,8,4096]{2,0,1:T(8,128)}, u32[]{:S(2)}) copy-start(f32[8,8,4096]{2,0,1:T(8,128)} %reshape.41) | copy-start | bytes 3145732

commit v5 on v4

--- a/solution.py
+++ b/solution.py
@@ -11,8 +11,9 @@
 TILE = 64
 SLAB_VIRT = 128
 LINE = 4
-CHUNKS = 4
+CHUNKS = 2
 PIECES = 2
+PAIR = 2
 STEP = 16
 WIDE = 512
 NARROW = 256
@@ -157,73 +158,78 @@
             device_id=(o, target), device_id_type=MESH,
         )
 
-    for c in range(CHUNKS):
-        spread(always, v, c, True, True, True, True)
-
     @pl.when(v == owner)
     def _():
         own_strip.start()
         for step in range(1, n_vir):
             far_strip(step).start()
-        own_strip.wait()
-
+
+    for c in range(CHUNKS):
+        spread(always, v, c, True, True, True, True)
     gathered[v] = main[...]
 
-    @pl.when(v != owner)
-    def _():
-        along(v, CHUNKS, False, 0, v).wait_recv()
-
-    spread(always, v, CHUNKS, True, True, True, True)
+    def phase(d, c):
+        if d < line:
+            arrive(z >= d, (z - d) * wide + x, c, True, False, True)
+            arrive(z < line - d, (z + d) * wide + x, c, False, True, True)
+        e = d - 1
+        for step in range(1, wide):
+            side = lax.rem(x + step, wide)
+            arrive(z >= e, (z - e) * wide + side, c, False, False, False)
+            if e:
+                arrive(z < line - e, (z + e) * wide + side, c, False, False, False)
 
     for d in range(1, line + 1):
-        for c in range(CHUNKS + 1):
-            if d < line:
-                arrive(z >= d, (z - d) * wide + x, c, True, False, True)
-                arrive(z < line - d, (z + d) * wide + x, c, False, True, True)
-            for step in range(1, wide):
-                side = lax.rem(x + step, wide)
-                e = d - 1
-                arrive(z >= e, (z - e) * wide + side, c, False, False, False)
-                if e:
-                    arrive(z < line - e, (z + e) * wide + side, c, False, False, False)
-            if d <= 2 and c < CHUNKS:
+        for c in range(CHUNKS):
+            phase(d, c)
+            if d <= 2:
                 if d == 1 and c == 0:
                     load.wait()
                 permute((d - 1) * CHUNKS + c, 2 * CHUNKS)
         if d == 1:
+            pl.when(v == owner)(own_strip.wait)
+
+            @pl.when(v != owner)
+            def _():
+                along(v, CHUNKS, False, 0, v).wait_recv()
+
+            spread(always, v, CHUNKS, True, True, True, True)
             group(z)
         else:
+            phase(d - 1, CHUNKS)
             pl.when(z >= d - 1)(lambda: group(z - d + 1))
             pl.when(z < line - d + 1)(lambda: group(z + d - 1))
+    phase(line, CHUNKS)
 
     multiply(lambda: gathered[n_vir], straight, [(0, owner)])
     turned[o, 0] = gathered[n_vir]
     for k in range(1, ratio):
         turned[o, k] = gathered[n_vir]
-    for step in range(1, n_occ):
-        other = lax.rem(o + step, n_occ)
-        for k in range(ratio):
-            for c in range(CHUNKS):
-                pltpu.make_async_remote_copy(
-                    src_ref=turned.at[other, k, pl.ds(c * piece, piece)],
-                    dst_ref=turned.at[other, k, pl.ds(c * piece, piece)],
-                    send_sem=turn_send.at[0, c], recv_sem=turn_recv.at[other, k, c],
-                    device_id=(o, v), device_id_type=MESH,
-                ).wait_recv()
     swap = pair_swap(cols)
-
-    @pl.loop(0, n_occ * ratio)
-    def _(at):
-        p, k = at // ratio, lax.rem(at, ratio)
-        moved = jnp.dot(swap, turned[p, k], preferred_element_type=jnp.float32)
-        turned[p, k] = moved.astype(jnp.bfloat16)
-
-    places = []
-    for p in range(n_occ):
-        for k in range(ratio):
-            s = jnp.where(p < o, k, 1 - k)
-            places.append((jnp.where(p == o, 1, k), p * ratio + jnp.where(p == o, 0, s)))
-    multiply(lambda: turned[...].reshape(n_occ * ratio * pairs, cdim), crossed, places)
+    for step in range(n_occ // PAIR):
+        base = lax.rem(o // PAIR + step, n_occ // PAIR) * PAIR
+        places = []
+        for p in [base + at for at in range(PAIR)]:
+            for k in range(ratio):
+
+                @pl.when(p != o)
+                def _(p=p, k=k):
+                    for c in range(CHUNKS):
+                        landed = turned.at[p, k, pl.ds(c * piece, piece)]
+                        pltpu.make_async_remote_copy(
+                            src_ref=landed, dst_ref=landed,
+                            send_sem=turn_send.at[0, c], recv_sem=turn_recv.at[p, k, c],
+                            device_id=(o, v), device_id_type=MESH,
+                        ).wait_recv()
+
+                moved = jnp.dot(swap, turned[p, k], preferred_element_type=jnp.float32)
+                turned[p, k] = moved.astype(jnp.bfloat16)
+                s = jnp.where(p < o, k, 1 - k)
+                places.append((jnp.where(p == o, 1, k), p * ratio + jnp.where(p == o, 0, s)))
+        multiply(
+            lambda base=base: turned[pl.ds(base, PAIR)].reshape(PAIR * ratio * pairs, cdim),
+            crossed, places,
+        )
     for cond, finish in waits:
         pl.when(cond)(finish)
 

time: 135 us -> 131 us (0.970)
  the two profiles are of different devices: /device:TPU:24 before, /device:TPU:0 now
where the time goes in v5:
time: 131 us
  Pallas kernels  89.1 us (68%)
  local copies, waits for them, and re-layouts  20 us (15%)
  waiting for transfers between devices  12.4 us (9%)
  other arithmetic  6.09 us (5%)
  starting transfers between devices  2.97 us (2%)
    pallas_call x1, Pallas kernels, ladder(): pl.pallas_call(functools.partial(exchange_kernel, n_occ, n_vir), out_shap...  89.1 us
    ppermute x2, waiting for transfers between devices, per_device(): got = lax.ppermute(sent[:, at:at + cut], ('occ', 'vir'), pairs)  12.4 us
    convert_element_type x9, local copies, waits for them, and re-layouts, add(): return (a.astype(jnp.float32) + b.astype(jnp.float32)).astype(jnp.bfloat16)  12 us
    unnamed x3, local copies, waits for them, and re-layouts  5.62 us
    ppermute x2, starting transfers between devices, per_device(): got = lax.ppermute(sent[:, at:at + cut], ('occ', 'vir'), pairs)  2.97 us
  transfers between devices with their start and end apart: 2, of which 2 were waited for; matrix products, arithmetic and copies ran while one was open for 7% of the time, Pallas kernels for 0%

profile of v5, /device:TPU:0, one launch (start us, length us, event | category | flops | bytes accessed | tf_op | source)
XLA Modules:
  0.0 130.6 jit_solution(17970020159701393762)
XLA Ops:
  0.0 0.7 convert_element_type.58
  0.7 2.4 %copy_multiply_fusion = bf16[16,8,4096]{2,0,1:T(8,128)(2,1)S(1)} fusion(bf16[16,8,4096]{2,1,0:T(8,128)(2,1)} %param.3, bf16[16,8]{0,1:T(8,128)(2,1)S(1)} %convert_element_type.58), kind=kLoop, calls=%fused_computation | loop fusion | flops 524288 | bytes 2097408 | tf_op jit(solution)/shard_map/mul | solution.py:292
  3.1 1.0 broadcast_select_fusion.1
  4.0 0.8 fusion.1
  4.8 2.9 %collective-permute-start.1 = (bf16[8,4,4096]{2,0,1:T(8,128)(2,1)}, bf16[8,4,4096]{2,0,1:T(8,128)(2,1)}, u32[]{:S(2)}, u32[]{:S(2)}) collective-permute-start(bf16[8,4,4096]{2,0,1:T(8,128)(2,1)} %get-tuple-element.13), channel_id=1, source_target_pairs={{0,1},{1,0},{2,9},{3,8},{4,17},{5,16},{6,25},{7,24},{8,2},{9,3},{1... | collective-permute-start | bytes 786440 | tf_op jit(solution)/shard_map/ppermute | solution.py:308
  7.8 0.0 collective-permute-start
  7.8 2.2 %reshape.44 = f32[8,8,64,64]{3,2,0,1:T(8,128)} reshape(f32[8,8,4096]{2,0,1:T(8,128)S(1)} %get-tuple-element.7) | data formatting | bytes 2097152 | tf_op jit(solution)/shard_map/convert_element_type | solution.py:278
  10.0 1.9 %copy.19 = f32[8,8,64,64]{2,3,1,0:T(8,128)S(1)} copy(f32[8,8,64,64]{3,2,0,1:T(8,128)} %reshape.44) | data formatting | bytes 2097152 | tf_op jit(solution)/shard_map/convert_element_type | solution.py:278
  11.9 1.6 %reshape.41 = f32[8,8,4096]{2,0,1:T(8,128)} reshape(f32[8,8,64,64]{3,2,0,1:T(8,128)S(1)} %bitcast.31) | data formatting | bytes 2097152 | tf_op jit(solution)/shard_map/convert_element_type | solution.py:278
  13.5 9.3 %collective-permute-done.1 = bf16[8,4,4096]{2,0,1:T(8,128)(2,1)} collective-permute-done((bf16[8,4,4096]{2,0,1:T(8,128)(2,1)}, bf16[8,4,4096]{2,0,1:T(8,128)(2,1)}, u32[]{:S(2)}, u32[]{:S(2)}) %collective-permute-start.1) | collective-permute-done | bytes 262176 | tf_op jit(solution)/shard_map/ppermute | solution.py:308
  22.8 1.4 %reshape.46 = f32[8,4,64,64]{3,2,0,1:T(8,128)S(1)} reshape(bf16[8,4,4096]{2,0,1:T(8,128)(2,1)} %collective-permute-done.1) | data formatting | bytes 786432 | tf_op jit(solution)/shard_map/convert_element_type | solution.py:278
  24.2 0.3 copy.27
  24.5 0.0 copy-start
  24.5 1.2 reshape.48
  25.8 3.1 %collective-permute-done = bf16[8,4,4096]{2,0,1:T(8,128)(2,1)S(1)} collective-permute-done((bf16[8,4,4096]{2,0,1:T(8,128)(2,1)}, bf16[8,4,4096]{2,0,1:T(8,128)(2,1)S(1)}, u32[]{:S(2)}, u32[]{:S(2)}) %collective-permute-start) | collective-permute-done | bytes 262176 | tf_op jit(solution)/shard_map/ppermute | solution.py:308
  28.8 0.4 reshape.45
  29.3 1.3 %copy.26 = f32[4,8,64,64]{3,2,0,1:T(8,128)} copy(f32[4,8,64,64]{2,3,1,0:T(8,128)S(1)} %bitcast.33) | data formatting | bytes 1048576 | tf_op jit(solution)/shard_map/convert_element_type | solution.py:278
  30.6 1.7 %reshape.47 = f32[4,8,4096]{2,0,1:T(4,128)S(1)} reshape(f32[4,8,64,64]{3,2,0,1:T(8,128)} %copy.26) | data formatting | bytes 1048576 | tf_op jit(solution)/shard_map/convert_element_type | solution.py:278
  32.2 1.7 %add_convert_fusion.2 = (bf16[4,8,4096]{2,0,1:T(4,128)(2,1)S(1)}, bf16[4,8,4096]{2,0,1:T(4,128)(2,1)S(1)}) fusion(f32[4,8,4096]{2,0,1:T(4,128)S(1)} %reshape.47, bf16[8,8,4096]{2,0,1:T(8,128)(2,1)} %get-tuple-element.5, f32[4,8,4096]{2,0,1:T(4,128)} %reshape.48), kind=kLoop, calls=%fused_computation.7 | loop fusion | flops 786432 | bytes 2097152 | tf_op jit(solution)/shard_map/convert_element_type | solution.py:278
  33.9 0.0 copy-done
  33.9 0.4 pad_maximum_fusion
  34.3 1.6 %copy_bitcast_fusion = (bf16[64,4096]{1,0:T(8,128)(2,1)}, bf16[64,4096]{1,0:T(8,128)(2,1)}) fusion(bf16[8,8,4096]{2,0,1:T(8,128)(2,1)S(1)} %get-tuple-element.8, bf16[8,8,4096]{2,0,1:T(8,128)(2,1)S(1)} %get-tuple-element.9), kind=kLoop, calls=%fused_computation.4 | loop fusion | bytes 2097152 | tf_op jit(solution)/shard_map/reshape | solution.py:315
  35.9 89.1 %shard_map.37 = bf16[16,8,8,2048]{3,2,1,0:T(8,128)(2,1)} custom-call(bf16[64,4096]{1,0:T(8,128)(2,1)} %get-tuple-element.15.main, bf16[64,4096]{1,0:T(8,128)(2,1)} %get-tuple-element.14.extra, bf16[64,64,2048]{2,1,0:T(8,128)(2,1)} %bitcast.35), custom_call_target="tpu_custom_call" | custom-call | flops 34359738368 | bytes 33554432 | tf_op jit(solution)/shard_map/pallas_call | solution.py:248
  125.0 5.6 %copy.30 = bf16[128,8,16,128]{3,2,1,0:T(8,128)(2,1)} copy(bf16[128,8,16,128]{3,1,2,0:T(8,128)(2,1)} %bitcast.34) | data formatting | bytes 8388608
Async XLA Ops:
  4.8 18.0 %collective-permute-start.1 = (bf16[8,4,4096]{2,0,1:T(8,128)(2,1)}, bf16[8,4,4096]{2,0,1:T(8,128)(2,1)}, u32[]{:S(2)}, u32[]{:S(2)}) collective-permute-start(bf16[8,4,4096]{2,0,1:T(8,128)(2,1)} %get-tuple-element.13), channel_id=1, source_target_pairs={{0,1},{1,0},{2,9},{3,8},{4,17},{5,16},{6,25},{7,24},{8,2},{9,3},{1... | collective-permute-start | bytes 786440 | tf_op jit(solution)/shard_map/ppermute | solution.py:308
  7.8 21.1 %collective-permute-start = (bf16[8,4,4096]{2,0,1:T(8,128)(2,1)}, bf16[8,4,4096]{2,0,1:T(8,128)(2,1)S(1)}, u32[]{:S(2)}, u32[]{:S(2)}) collective-permute-start(bf16[8,4,4096]{2,0,1:T(8,128)(2,1)} %get-tuple-element.12), channel_id=1, source_target_pairs={{0,1},{1,0},{2,9},{3,8},{4,17},{5,16},{6,25},{7,24},{8,2},{9,3},{1... | collective-permute-start | bytes 786440 | tf_op jit(solution)/shard_map/ppermute | solution.py:308
  24.5 9.4 %copy-start = (f32[8,8,4096]{2,0,1:T(8,128)S(1)}, f32[8,8,4096]{2,0,1:T(8,128)}, u32[]{:S(2)}) copy-start(f32[8,8,4096]{2,0,1:T(8,128)} %reshape.41) | copy-start | bytes 3145732
